TPU v7x, 32 devices: a whole 2x2x4 slice. The times are simulated.
32 devices in a mesh: groups: 2 (over x), attn: 8 (over z, y), exp: 2 (over core).
Axes of the slice: x: 2, y: 2, z: 4, core: 2. Of those that a mesh axis runs over, the one named last changes fastest.
Arguments:
- queries: bfloat16 [192, 6144], P(('groups', 'attn'), 'exp'), parts along dimension 0, may hold values from -6 to 6
- new_keys: bfloat16 [192, 1024], P(('groups', 'attn'), 'exp'), parts along dimension 0, may hold values from -6 to 6
- new_values: bfloat16 [192, 1024], P(('groups', 'attn'), 'exp'), parts along dimension 0, may hold values from -6 to 6
- key_cache: bfloat16 [192, 128, 1024], P(('groups', 'attn'), None, 'exp'), parts along dimension 0, may hold values from -6 to 6
- value_cache: bfloat16 [192, 128, 1024], P(('groups', 'attn'), None, 'exp'), parts along dimension 0, may hold values from -6 to 6
- cache_lengths: int32 [192], P(('groups', 'attn')), parts along dimension 0, may hold values from 1 to 128, as said below
- tokens: bfloat16 [192, 6144], P(('groups', 'attn')), parts along dimension 0, may hold values from -6 to 6
- expert_ids: int32 [192, 2], P(('groups', 'attn')), parts along dimension 0, may hold values from 0 to 3, all different within a row; in each aligned block of 12 rows (0 to 11, 12 to 23, ...) at most 8 rows name the same one
- gate_weights: float32 [192, 2], P(('groups', 'attn')), parts along dimension 0, may hold values from 0.2 to 1
- w_gate: bfloat16 [6144, 32768], P(None, ('attn', 'exp')), may hold values from -0.078125 to 0.078125
- w_up: bfloat16 [6144, 32768], P(None, ('attn', 'exp')), may hold values from -0.078125 to 0.078125
- w_down: bfloat16 [32768, 6144], P(('attn', 'exp')), may hold values from -0.0625 to 0.0625
Outputs:
- context: bfloat16 [192, 6144], P(('groups', 'attn'), 'exp'), parts along dimension 0
- expert_out: bfloat16 [192, 6144], P(('groups', 'attn')), parts along dimension 0
There are 2 independent parts, one for each index of `groups`. A program takes and returns all parts, laid end to end along the dimension named above; an argument that names none is the same for every part. Nothing has to cross between parts.
Inputs may be any that keep to these rules, and one draw needn't show every extreme that they name: Each row attends to its first cache_lengths cached positions and to its new key. `expert_ids`: the two experts of a row differ; in the rows of one index of attn no expert is named more than 8 times, and that number is reached.
All inputs are finite; a program needn't handle non-finite values.
Results may differ from a plain program's by a relative error of at most 0.0058.
Values may be sent and summed in bfloat16 or wider, within the bound.
A program may use at most 192 MiB of HBM per device.

v0:
```python
import jax
import jax.numpy as jnp
from jax import lax
from jax.sharding import PartitionSpec as P

HEAD_DIM = 128
EXPERTS = 4
CAPACITY = 8


def attend(queries, new_keys, new_values, key_cache, value_cache, cache_lengths):
    row_count = queries.shape[0]
    cache_len = key_cache.shape[1]
    kv_groups = key_cache.shape[2] // HEAD_DIM
    shared = queries.shape[1] // (kv_groups * HEAD_DIM)
    grouped = queries.reshape(row_count, kv_groups, shared, HEAD_DIM)
    key_heads = key_cache.reshape(row_count, cache_len, kv_groups, HEAD_DIM)
    value_heads = value_cache.reshape(row_count, cache_len, kv_groups, HEAD_DIM)
    own_keys = new_keys.reshape(row_count, kv_groups, HEAD_DIM)
    own_values = new_values.reshape(row_count, kv_groups, 1, HEAD_DIM).astype(jnp.float32)
    softmax_scale = HEAD_DIM ** (-0.5)
    cached = (
        jnp.einsum("rgjd,rlgd->rgjl", grouped, key_heads, preferred_element_type=jnp.float32)
        * softmax_scale
    )
    own_score = (
        jnp.einsum("rgjd,rgd->rgj", grouped, own_keys, preferred_element_type=jnp.float32)
        * softmax_scale
    )
    usable = (
        jnp.arange(cache_len, dtype=jnp.int32)[None, None, None, :]
        < cache_lengths[:, None, None, None]
    )
    cached = jnp.where(usable, cached, -1e30)
    highest = jnp.maximum(jnp.max(cached, axis=3), own_score)
    lifted = jnp.where(usable, jnp.exp(cached - highest[..., None]), 0.0)
    lifted_own = jnp.exp(own_score - highest)
    denominator = jnp.sum(lifted, axis=3) + lifted_own
    weights = (lifted / denominator[..., None]).astype(jnp.bfloat16)
    weight_own = (lifted_own / denominator).astype(jnp.bfloat16)
    mixed = jnp.einsum("rgjl,rlgd->rgjd", weights, value_heads, preferred_element_type=jnp.float32)
    mixed = mixed + weight_own[..., None].astype(jnp.float32) * own_values
    return mixed.reshape(row_count, kv_groups * shared * HEAD_DIM).astype(jnp.bfloat16)


def route_slots(expert_ids, block, count):
    row_count = expert_ids.shape[0]
    matches = (expert_ids[:, :, None] == jnp.arange(count, dtype=jnp.int32)[None, None, :]).astype(
        jnp.int32
    )
    per_row = jnp.sum(matches, axis=1).reshape(row_count // block, block, count)
    before = (jnp.cumsum(per_row, axis=1) - per_row).reshape(row_count, count)
    return jnp.sum(matches * before[:, None, :], axis=2)


def per_device(
    queries,
    new_keys,
    new_values,
    key_cache,
    value_cache,
    cache_lengths,
    tokens,
    expert_ids,
    gate_weights,
    w_gate,
    w_up,
    w_down,
):
    context = attend(queries, new_keys, new_values, key_cache, value_cache, cache_lengths)
    row_count, model_width = tokens.shape
    slot_pos = route_slots(expert_ids, row_count, EXPERTS)
    slot_index = expert_ids * CAPACITY + slot_pos
    targets = jnp.arange(EXPERTS * CAPACITY, dtype=jnp.int32)
    matches = slot_index[:, :, None] == targets[None, None, :]
    selector = jnp.any(matches, axis=1).T.astype(jnp.bfloat16)
    outgoing = jnp.dot(selector, tokens, preferred_element_type=jnp.float32).astype(jnp.bfloat16)
    outgoing = outgoing.reshape(EXPERTS, CAPACITY, model_width)
    attn_devices = lax.axis_size("attn")
    core_count = lax.axis_size("exp")
    half_slots = CAPACITY // core_count
    fanned = jnp.repeat(outgoing, attn_devices // EXPERTS, axis=0)
    received = lax.all_to_all(fanned, "attn", split_axis=0, concat_axis=0, tiled=True)
    flat_rows = received.reshape(attn_devices * CAPACITY, model_width)
    gate_pre = jnp.dot(flat_rows, w_gate, preferred_element_type=jnp.float32)
    up_pre = jnp.dot(flat_rows, w_up, preferred_element_type=jnp.float32)
    hidden = (jax.nn.silu(gate_pre) * up_pre).astype(jnp.bfloat16)
    partial_out = jnp.dot(hidden, w_down, preferred_element_type=jnp.float32)
    partial_out = partial_out.reshape(attn_devices, core_count, half_slots, model_width)
    group_share = lax.psum_scatter(partial_out, "exp", scatter_dimension=1, tiled=True).astype(
        jnp.bfloat16
    )
    combiner = jnp.sum(gate_weights[:, :, None] * matches.astype(jnp.float32), axis=1)
    both = lax.all_gather(group_share, "exp", axis=1, tiled=True)
    outbound = both.reshape(attn_devices, CAPACITY, model_width)
    returned = lax.all_to_all(outbound, "attn", split_axis=0, concat_axis=0, tiled=True)
    summed = jnp.sum(
        returned.astype(jnp.float32).reshape(
            EXPERTS, attn_devices // EXPERTS, CAPACITY, model_width
        ),
        axis=1,
    )
    combined = jnp.dot(
        combiner, summed.reshape(EXPERTS * CAPACITY, model_width), precision=lax.Precision.HIGHEST
    )
    return (context, combined.astype(jnp.bfloat16))


def solution(mesh):
    placed = (
        P(("groups", "attn"), "exp"),
        P(("groups", "attn"), "exp"),
        P(("groups", "attn"), "exp"),
        P(("groups", "attn"), None, "exp"),
        P(("groups", "attn"), None, "exp"),
        P(("groups", "attn")),
        P(("groups", "attn"), None),
        P(("groups", "attn"), None),
        P(("groups", "attn"), None),
        P(None, ("attn", "exp")),
        P(None, ("attn", "exp")),
        P(("attn", "exp"), None),
    )
    return jax.shard_map(
        per_device,
        mesh=mesh,
        in_specs=placed,
        out_specs=(P(("groups", "attn"), "exp"), P(("groups", "attn"), None)),
        check_vma=False,
    )
```

profile of v0, /device:TPU:0, one launch (start us, length us, event | category | flops | bytes accessed | tf_op | source)
XLA Modules:
  0.0 121.2 jit_solution(10175273150904055403)
XLA Ops:
  7.2 0.0 copy-start
  7.2 0.0 reduce-scatter.2.cloned.1.call-start
  7.2 0.8 convert_reduce_fusion.1
  8.0 0.2 reduce_window_sum.11
  8.2 0.7 select_reduce_fusion.1
  8.9 0.7 multiply_add_fusion
  9.6 0.1 fusion.37
  9.7 1.2 %fusion = bf16[4,8,6144]{2,1,0:T(8,128)(2,1)S(1)} fusion(pred[12,32]{1,0:T(8,128)(4,1)S(1)} %fusion.37, bf16[12,6144]{1,0:T(8,128)(2,1)} %param.18), kind=kOutput, calls=%fused_computation.1 | convolution fusion | flops 4915200 | bytes 541056 | tf_op jit(solution)/shard_map/dot_general | solution.py:77
  10.9 0.1 broadcast_in_dim.34
  11.0 27.2 %all_to_all.10 = bf16[8,8,6144]{2,1,0:T(8,128)(2,1)S(1)} all-to-all(bf16[8,8,6144]{2,1,0:T(8,128)(2,1)S(1)} %bitcast.51), channel_id=1, replica_groups=mesh['groups'=2,'attn'=8,'exp'=2] {'attn'}, dimensions={0} | all-to-all | bytes 1572864 | tf_op jit(solution)/shard_map/all_to_all | solution.py:83
  38.2 10.5 %fusion.24 = f32[64,2048]{1,0:T(8,128)S(1)} fusion(bf16[6144,2048]{1,0:T(8,128)(2,1)} %param.21, bf16[8,8,6144]{2,1,0:T(8,128)(2,1)S(1)} %all_to_all.10), kind=kOutput, calls=%fused_computation.19 | convolution fusion | flops 1610612736 | bytes 26476544 | tf_op jit(solution)/shard_map/dot_general | solution.py:85
  48.7 21.0 %fusion.2 = f32[64,6144]{1,0:T(8,128)} fusion(bf16[2048,6144]{1,0:T(8,128)(2,1)} %param.23, bf16[6144,2048]{1,0:T(8,128)(2,1)} %param.22, bf16[8,8,6144]{2,1,0:T(8,128)(2,1)S(1)} %all_to_all.10, f32[64,2048]{1,0:T(8,128)S(1)} %fusion.24), kind=kOutput, calls=%fused_computation.5 | convolution fusion | flops 3222011904 | bytes 53215232 | tf_op jit(solution)/shard_map/dot_general | solution.py:88
  69.7 1.8 %reshape.101 = f32[8,2,4,6144]{3,2,1,0:T(4,128)S(1)} reshape(f32[64,6144]{1,0:T(8,128)} %fusion.2) | data formatting | bytes 3145728 | tf_op jit(solution)/shard_map/reshape | solution.py:89
  71.5 2.1 %copy.50 = f32[8,2,4,6144]{3,0,2,1:T(8,128)} copy(f32[8,2,4,6144]{3,2,1,0:T(4,128)S(1)} %reshape.101) | data formatting | bytes 3145728 | tf_op jit(solution)/shard_map/reshape | solution.py:89
  73.6 0.0 reduce-scatter.2.cloned.1.call-update
  73.6 0.9 copy-done.1
  74.5 0.1 reshape.94
  74.6 0.2 fusion.43
  74.8 7.0 %reduce-scatter.2.cloned.1.call-done = f32[8,1,4,6144]{3,0,2,1:T(8,128)} async-done(((f32[8,2,4,6144]{3,0,2,1:T(8,128)}), f32[8,1,4,6144]{3,0,2,1:T(8,128)}) %reduce-scatter.2.cloned.1.call-update) | async-done | bytes 786448 | tf_op jit(solution)/shard_map/reduce_scatter | solution.py:90
  81.8 1.2 convert_element_type.55
  83.0 2.4 %all_gather.3 = bf16[8,2,4,6144]{3,0,2,1:T(8,128)(2,1)S(1)} all-gather(bf16[8,1,4,6144]{3,0,2,1:T(8,128)(2,1)S(1)} %convert_element_type.55), channel_id=1, replica_groups=mesh['groups'=2,'attn'=8,'exp'=2] {'exp'}, dimensions={1}, use_global_device_ids=true | all-gather | bytes 1179648 | tf_op jit(solution)/shard_map/all_gather | solution.py:94
  85.3 1.3 %copy.51 = bf16[8,8,6144]{2,1,0:T(8,128)(2,1)} copy(bf16[8,8,6144]{2,0,1:T(8,128)(2,1)S(1)} %bitcast.52) | data formatting | bytes 1572864 | tf_op jit(solution)/shard_map/reshape | solution.py:95
  86.7 5.8 %all-to-all-start.1 = ((bf16[8,8,6144]{2,1,0:T(8,128)(2,1)}), bf16[8,8,6144]{2,1,0:T(8,128)(2,1)S(1)}, u32[]{:S(2)}, u32[]{:S(2)}) async-start(bf16[8,8,6144]{2,1,0:T(8,128)(2,1)} %copy.51), calls=%async_computation.2 | async-start | bytes 1572864 | tf_op jit(solution)/shard_map/all_to_all | solution.py:96
  92.5 0.1 iota_compare_fusion.1
  92.6 1.0 fusion.42
  93.6 0.3 fusion.32
  93.9 0.6 fusion.18
  94.5 0.7 convert_element_type.51
  95.3 0.1 select_reduce_fusion
  95.4 17.7 %all-to-all-done.1 = bf16[8,8,6144]{2,1,0:T(8,128)(2,1)S(1)} async-done(((bf16[8,8,6144]{2,1,0:T(8,128)(2,1)}), bf16[8,8,6144]{2,1,0:T(8,128)(2,1)S(1)}, u32[]{:S(2)}, u32[]{:S(2)}) %all-to-all-start.1) | async-done | bytes 786464 | tf_op jit(solution)/shard_map/all_to_all | solution.py:96
  113.1 0.1 convert_reduce_fusion
  113.2 1.2 convolution_convert_fusion.1
  (17 shorter events, 0.1 us)
Async XLA Ops:
  7.2 85.4 %copy-start = (bf16[12,128,512]{2,1,0:T(8,128)(2,1)S(1)}, bf16[12,128,512]{2,1,0:T(8,128)(2,1)}, u32[]{:S(2)}) copy-start(bf16[12,128,512]{2,1,0:T(8,128)(2,1)} %param.15) | copy-start | bytes 4718596
  7.2 74.6 %reduce-scatter.2.cloned.1.call-start = ((), (), s32[]{:S(2)}) async-start(), calls=%async_computation.3 | async-start | bytes 2359296 | tf_op jit(solution)/shard_map/reduce_scatter | solution.py:90
  73.6 0.9 copy-start.1
  73.6 1.0 copy-start.2
  73.6 1.0 copy-start.3
  85.3 7.1 %copy-start.5 = (s32[12]{0:T(128)S(1)}, s32[12]{0:T(128)}, u32[]{:S(2)}) copy-start(s32[12]{0:T(128)} %param.17) | copy-start | bytes 148
  86.7 26.4 %all-to-all-start.1 = ((bf16[8,8,6144]{2,1,0:T(8,128)(2,1)}), bf16[8,8,6144]{2,1,0:T(8,128)(2,1)S(1)}, u32[]{:S(2)}, u32[]{:S(2)}) async-start(bf16[8,8,6144]{2,1,0:T(8,128)(2,1)} %copy.51), calls=%async_computation.2 | async-start | bytes 1572864 | tf_op jit(solution)/shard_map/all_to_all | solution.py:96
  92.5 1.4 %copy-start.6 = (bf16[12,128,512]{2,1,0:T(8,128)(2,1)S(1)}, bf16[12,128,512]{2,1,0:T(8,128)(2,1)}, u32[]{:S(2)}) copy-start(bf16[12,128,512]{2,1,0:T(8,128)(2,1)} %param.16) | copy-start | bytes 4718596
  93.9 1.4 %copy-start.4 = (f32[12,2]{0,1:T(2,128)S(1)}, f32[12,2]{0,1:T(2,128)}, u32[]{:S(2)}) copy-start(f32[12,2]{0,1:T(2,128)} %param.20) | copy-start | bytes 292
Sparse Core Ops, SparseCore 0:
  73.7 8.0 reduce-scatter.1
where the time goes:
time: 122 us; the launch traced here: 121 us
  matrix products  35.7 us (29%)
  blocking collectives  29.6 us (24%)
  waiting for transfers between devices  24.7 us (20%)
  between operations  14.2 us (12%)
  local copies, waits for them, and re-layouts  7.02 us (6%)
  starting transfers between devices  5.87 us (5%)
  other arithmetic  4.21 us (3%)
    all_to_all x1, blocking collectives, per_device(): lax.all_to_all(fanned, 'attn', split_axis=0, concat_axis=0, tiled=True)  27.2 us
    dot_general x1, matrix products, per_device(): partial_out = jnp.dot(hidden, w_down, preferred_element_type=jnp.float32)  21 us
    all_to_all x1, waiting for transfers between devices, per_device(): lax.all_to_all(outbound, 'attn', split_axis=0, concat_axis=0, tiled=True)  17.7 us
    dot_general x1, matrix products, per_device(): gate_pre = jnp.dot(flat_rows, w_gate, preferred_element_type=jnp.float32)  10.5 us
    reduce_scatter x1, waiting for transfers between devices, per_device(): lax.psum_scatter(partial_out, 'exp', scatter_dimension=1, tiled=True)  7 us
    all_to_all x1, starting transfers between devices, per_device(): lax.all_to_all(outbound, 'attn', split_axis=0, concat_axis=0, tiled=True)  5.83 us
    reshape x2, local copies, waits for them, and re-layouts, per_device(): partial_out.reshape(attn_devices, core_count, half_slots, model_width)  3.86 us
  transfers between devices with their start and end apart: 2, of which 2 were waited for; matrix products, arithmetic and copies ran while one was open for 3% of the time, Pallas kernels for 0%

commit v1 on v0

--- a/solution.py
+++ b/solution.py
@@ -1,11 +1,19 @@
+import functools
+
 import jax
 import jax.numpy as jnp
 from jax import lax
+from jax.experimental import pallas as pl
+from jax.experimental.pallas import tpu as pltpu
 from jax.sharding import PartitionSpec as P
 
 HEAD_DIM = 128
 EXPERTS = 4
 CAPACITY = 8
+MESH = pl.DeviceIdType.MESH
+RING = 18
+TILE = 512
+DEPTH = 2048
 
 
 def attend(queries, new_keys, new_values, key_cache, value_cache, cache_lengths):
@@ -106,6 +114,399 @@
     return (context, combined.astype(jnp.bfloat16))
 
 
+def attention_rows(lengths, qs, nkf, nvf, keys, values, os, first, count):
+    heads = qs.shape[1]
+    width = keys.shape[2]
+    kv = width // HEAD_DIM
+    shared = heads // kv
+    cached = keys.shape[1]
+    scale = HEAD_DIM ** (-0.5)
+    row_id = lax.broadcasted_iota(jnp.int32, (heads, HEAD_DIM), 0)
+    mine = [(row_id >= g * shared) & (row_id < (g + 1) * shared) for g in range(kv)]
+    lane = lax.broadcasted_iota(jnp.int32, (heads, cached), 1)
+
+    def pick(parts):
+        total = jnp.where(mine[0], parts[0], 0.0)
+        for g in range(1, kv):
+            total = jnp.where(mine[g], parts[g], total)
+        return total
+
+    for step in range(count):
+        r = first + step
+        q = qs[r]
+        spread = jnp.concatenate([jnp.where(m, q, 0.0) for m in mine], axis=1).astype(jnp.bfloat16)
+        s = lax.dot_general(
+            spread, keys[r], (((1,), (1,)), ((), ())), preferred_element_type=jnp.float32
+        ) * scale
+        usable = lane < lengths[r]
+        s = jnp.where(usable, s, -1e30)
+        nk = nkf[pl.ds(r, 1), :]
+        nv = nvf[pl.ds(r, 1), :]
+        cut = [slice(g * HEAD_DIM, (g + 1) * HEAD_DIM) for g in range(kv)]
+        own_key = pick([jnp.broadcast_to(nk[:, k], (heads, HEAD_DIM)) for k in cut])
+        own_value = pick([jnp.broadcast_to(nv[:, k], (heads, HEAD_DIM)) for k in cut])
+        own = jnp.sum(q * own_key, axis=1, keepdims=True) * scale
+        highest = jnp.maximum(jnp.max(s, axis=1, keepdims=True), own)
+        lifted = jnp.where(usable, jnp.exp(s - highest), 0.0)
+        lifted_own = jnp.exp(own - highest)
+        den = jnp.sum(lifted, axis=1, keepdims=True) + lifted_own
+        w = (lifted / den).astype(jnp.bfloat16)
+        w_own = (lifted_own / den).astype(jnp.bfloat16).astype(jnp.float32)
+        o = jnp.dot(w, values[r], preferred_element_type=jnp.float32)
+        os[r] = pick([o[:, k] for k in cut]) + w_own * own_value
+
+
+def layer_kernel(
+    attn_count,
+    lengths,
+    queries,
+    new_keys,
+    new_values,
+    key_cache,
+    value_cache,
+    tokens,
+    expert_ids,
+    gate_weights,
+    w_gate,
+    w_up,
+    w_down,
+    context,
+    expert_out,
+    q_v, nk_v, nv_v, k_v, v_v, tok_v, ids_v, gw_v,
+    qs, nkf, nvf, os, ctx_v,
+    outbuf, near, far, x, hid, ring,
+    psend, pgot, tf, tb, yb, zf, zb, home, comb_v, ob,
+    in_sem, ring_sem, put_sem,
+    d_s, d_r, fy_s, fy_r, fs_s, fs_r,
+    p_s, p_r, y_s, y_r, h_s, h_r, o_s, o_r,
+):
+    group = attn_count // EXPERTS
+    a = lax.axis_index("attn")
+    c = lax.axis_index("exp")
+    ex, j = a // group, a % group
+    rows, width = tok_v.shape
+    half = width // 2
+    hidden = hid.shape[1]
+    k_parts = width // DEPTH
+    n_blocks = hidden // TILE
+    out_blocks = half // TILE
+    per_block = 2 * k_parts
+
+    pairs = [
+        (tokens, tok_v), (expert_ids, ids_v), (gate_weights, gw_v), (queries, q_v),
+        (new_keys, nk_v), (new_values, nv_v), (key_cache, k_v), (value_cache, v_v),
+    ]
+    loads = [pltpu.make_async_copy(s, d, in_sem.at[n]) for n, (s, d) in enumerate(pairs)]
+    for load in loads:
+        load.start()
+
+    def up_tile(n, k, w):
+        t = n * per_block + k * 2 + w
+        slot = t % RING
+        source = w_up if w else w_gate
+        return slot, pltpu.make_async_copy(
+            source.at[pl.ds(k * DEPTH, DEPTH), pl.ds(pl.multiple_of(n * TILE, TILE), TILE)],
+            ring.at[slot],
+            ring_sem.at[slot],
+        )
+
+    def down_tile(i, own):
+        t = n_blocks * per_block + i * 2 + own
+        slot = t % RING
+        side = c if own else 1 - c
+        first = pl.multiple_of((side * out_blocks + i) * TILE, TILE)
+        return slot, pltpu.make_async_copy(
+            w_down.at[:, pl.ds(first, TILE)], ring.at[slot], ring_sem.at[slot]
+        )
+
+    ahead = RING // per_block
+
+    def prefetch(n, carry):
+        for k in range(k_parts):
+            for w in range(2):
+                up_tile(n, k, w)[1].start()
+        return carry
+
+    lax.fori_loop(0, ahead, prefetch, 0)
+
+    z_peer = [((ex + d) % EXPERTS) * group + j for d in range(EXPERTS)]
+    y_peer = [ex * group + (j + d) % group for d in range(group)]
+    barrier = pltpu.get_barrier_semaphore()
+    for peer in z_peer[1:] + y_peer[1:]:
+        pl.semaphore_signal(barrier, inc=1, device_id={"attn": peer}, device_id_type=MESH)
+    pl.semaphore_signal(barrier, inc=1, device_id={"exp": 1 - c}, device_id_type=MESH)
+
+    for load in loads[:3]:
+        load.wait()
+    ids = ids_v[...]
+    gates = gw_v[...]
+    spots = EXPERTS * CAPACITY
+    lane = lax.broadcasted_iota(jnp.int32, (rows, spots), 1)
+    row_id = lax.broadcasted_iota(jnp.int32, (rows, spots), 0)
+    lane_expert, lane_slot = lane // CAPACITY, lane % CAPACITY
+    first = ids[:, 0:1] == lane_expert
+    second = ids[:, 1:2] == lane_expert
+    routed = jnp.where(first | second, 1, 0)
+    before = jnp.zeros((rows, spots), jnp.int32)
+    for r in range(rows - 1):
+        before = before + jnp.where(row_id > r, routed[r : r + 1, :], 0)
+    chosen = (routed > 0) & (before == lane_slot)
+    comb_v[...] = jnp.where(chosen, jnp.where(first, gates[:, 0:1], gates[:, 1:2]), 0.0)
+    selector = jnp.where(chosen, 1.0, 0.0).astype(jnp.bfloat16)
+    mine = tok_v[:, pl.ds(pl.multiple_of(c * half, half), half)]
+    outgoing = lax.dot_general(
+        selector, mine, (((0,), (0,)), ((), ())), preferred_element_type=jnp.float32
+    )
+    outbuf[...] = outgoing.reshape(EXPERTS, CAPACITY, half).astype(jnp.bfloat16)
+    pl.semaphore_wait(barrier, EXPERTS + group - 1)
+
+    def remote(src, dst, s_sem, r_sem, device):
+        return pltpu.make_async_remote_copy(
+            src_ref=src, dst_ref=dst, send_sem=s_sem, recv_sem=r_sem,
+            device_id=device, device_id_type=MESH,
+        )
+
+    sends = []
+    for d in range(1, EXPERTS):
+        e2 = (ex + d) % EXPERTS
+        cp = remote(
+            outbuf.at[e2], near.at[j * EXPERTS + ex], d_s.at[d], d_r.at[ex], {"attn": z_peer[d]}
+        )
+        cp.start()
+        sends.append(cp)
+    near[j * EXPERTS + ex] = outbuf[ex]
+
+    for load in loads[3:]:
+        load.wait()
+    heads = qs.shape[1]
+    for h in range(heads):
+        qs[:, h, :] = q_v[:, h * HEAD_DIM : (h + 1) * HEAD_DIM].astype(jnp.float32)
+    nkf[...] = nk_v[...].astype(jnp.float32)
+    nvf[...] = nv_v[...].astype(jnp.float32)
+    at_once = 4 if rows % 4 == 0 else 1
+
+    def attend_some(n, carry):
+        attention_rows(lengths, qs, nkf, nvf, k_v, v_v, os, n * at_once, at_once)
+        return carry
+
+    def pass_on(place, e, direct):
+        if direct:
+            for d in range(1, group):
+                cp = remote(
+                    near.at[place], near.at[place], fy_s.at[e, d], fy_r.at[place],
+                    {"attn": y_peer[d]},
+                )
+                cp.start()
+                sends.append(cp)
+        cp = remote(near.at[place], far.at[place], fs_s.at[place], fs_r.at[place], {"exp": 1 - c})
+        cp.start()
+        sends.append(cp)
+
+    pass_on(j * EXPERTS + ex, ex, True)
+    lax.fori_loop(0, rows // at_once, attend_some, 0)
+    for d in range(1, EXPERTS):
+        e2 = (ex + EXPERTS - d) % EXPERTS
+        place = j * EXPERTS + e2
+        remote(near.at[place], near.at[place], d_s.at[d], d_r.at[e2], {"exp": 1 - c}).wait_recv()
+        pass_on(place, e2, True)
+    for h in range(heads):
+        ctx_v[:, h * HEAD_DIM : (h + 1) * HEAD_DIM] = os[:, h, :].astype(jnp.bfloat16)
+    put_context = pltpu.make_async_copy(ctx_v, context, put_sem.at[0])
+    put_context.start()
+    for m in range(1, group):
+        j2 = (j + m) % group
+        for d in range(EXPERTS):
+            e2 = (ex + EXPERTS - d) % EXPERTS
+            place = j2 * EXPERTS + e2
+            remote(
+                near.at[place], near.at[place], fy_s.at[e2, m], fy_r.at[place], {"exp": 1 - c}
+            ).wait_recv()
+            pass_on(place, e2, False)
+    for place in range(attn_count):
+        remote(
+            near.at[place], far.at[place], fs_s.at[place], fs_r.at[place], {"exp": 1 - c}
+        ).wait_recv()
+    slots = attn_count * CAPACITY
+    x[:, pl.ds(pl.multiple_of(c * half, half), half)] = (
+        near[...].astype(jnp.float32).reshape(slots, half).astype(jnp.bfloat16)
+    )
+    x[:, pl.ds(pl.multiple_of((1 - c) * half, half), half)] = (
+        far[...].astype(jnp.float32).reshape(slots, half).astype(jnp.bfloat16)
+    )
+
+    def hidden_block(n, carry):
+        sums = [None, None]
+        for k in range(k_parts):
+            for w in range(2):
+                slot, tile = up_tile(n, k, w)
+                tile.wait()
+                term = jnp.dot(
+                    x[:, k * DEPTH : (k + 1) * DEPTH], ring[slot],
+                    preferred_element_type=jnp.float32,
+                )
+                sums[w] = term if k == 0 else sums[w] + term
+
+                @pl.when(n + ahead < n_blocks)
+                def _():
+                    up_tile(n + ahead, k, w)[1].start()
+
+                later = (n + ahead - n_blocks) * k_parts + k
+
+                @pl.when((n + ahead >= n_blocks) & (later < out_blocks))
+                def _():
+                    down_tile(later, w)[1].start()
+
+        g, u = sums
+        act = g / (1.0 + jnp.exp(-g)) * u
+        hid[:, pl.ds(pl.multiple_of(n * TILE, TILE), TILE)] = act.astype(jnp.bfloat16)
+        return carry
+
+    lax.fori_loop(0, n_blocks, hidden_block, 0)
+
+    def sibling(i):
+        return remote(psend.at[i], pgot.at[i], p_s.at[i], p_r.at[i], {"exp": 1 - c})
+
+    def across(i, d):
+        j2 = (j + d) % group
+        return remote(tb.at[i, j2], yb.at[i, j], y_s.at[i, d], y_r.at[i, j], {"attn": y_peer[d]})
+
+    def to_home(i, d):
+        e2 = (ex + d) % EXPERTS
+        return remote(zb.at[i, e2], home.at[i, ex], h_s.at[i, d], h_r.at[i, ex], {"attn": z_peer[d]})
+
+    def finish(i):
+        total = zf[i]
+        for d in range(1, group):
+            j2 = (j + d) % group
+            remote(
+                tb.at[i, j2], yb.at[i, j2], y_s.at[i, d], y_r.at[i, j2], {"exp": 1 - c}
+            ).wait_recv()
+            total = total + yb[i, j2].astype(jnp.float32).reshape(EXPERTS * CAPACITY, TILE)
+        zb[i] = total.reshape(EXPERTS, CAPACITY, TILE).astype(jnp.bfloat16)
+        for d in range(1, EXPERTS):
+            to_home(i, d).start()
+        home[i, ex] = zb[i, ex]
+
+    def down_block(i, carry):
+        slot, tile = down_tile(i, 0)
+        tile.wait()
+        psend[i] = jnp.dot(hid[...], ring[slot], preferred_element_type=jnp.float32)
+        sibling(i).start()
+        slot, tile = down_tile(i, 1)
+        tile.wait()
+        mine = jnp.dot(hid[...], ring[slot], preferred_element_type=jnp.float32)
+
+        @pl.when(i > 0)
+        def _():
+            finish(i - 1)
+
+        sibling(i).wait_recv()
+        mine = mine + pgot[i]
+        tf[...] = mine.reshape(group, EXPERTS * CAPACITY, TILE)
+        tb[i] = mine.reshape(group, EXPERTS, CAPACITY, TILE).astype(jnp.bfloat16)
+        zf[i] = tf[j]
+        for d in range(1, group):
+            across(i, d).start()
+        return carry
+
+    lax.fori_loop(0, out_blocks, down_block, 0)
+    finish(out_blocks - 1)
+
+    def combine(i, carry):
+        for d in range(1, EXPERTS):
+            e2 = (ex + d) % EXPERTS
+            remote(
+                zb.at[i, e2], home.at[i, e2], h_s.at[i, d], h_r.at[i, e2], {"exp": 1 - c}
+            ).wait_recv()
+        ob[:, pl.ds(pl.multiple_of(i * TILE, TILE), TILE)] = jnp.dot(
+            comb_v[...], home[i].astype(jnp.float32).reshape(spots, TILE),
+            precision=lax.Precision.HIGHEST, preferred_element_type=jnp.float32,
+        ).astype(jnp.bfloat16)
+        return carry
+
+    lax.fori_loop(0, out_blocks, combine, 0)
+    own_columns = pl.ds(pl.multiple_of(c * half, half), half)
+    give = remote(ob, expert_out.at[:, own_columns], o_s, o_r, {"exp": 1 - c})
+    give.start()
+    put_out = pltpu.make_async_copy(ob, expert_out.at[:, own_columns], put_sem.at[1])
+    put_out.start()
+    for cp in sends:
+        cp.wait_send()
+
+    def drain(i, carry):
+        sibling(i).wait_send()
+        for d in range(1, group):
+            across(i, d).wait_send()
+        for d in range(1, EXPERTS):
+            to_home(i, d).wait_send()
+        return carry
+
+    lax.fori_loop(0, out_blocks, drain, 0)
+    put_context.wait()
+    put_out.wait()
+    other_columns = pl.ds(pl.multiple_of((1 - c) * half, half), half)
+    give.wait_send()
+    remote(ob, expert_out.at[:, other_columns], o_s, o_r, {"exp": 1 - c}).wait_recv()
+
+
+def fused(
+    queries, new_keys, new_values, key_cache, value_cache, cache_lengths,
+    tokens, expert_ids, gate_weights, w_gate, w_up, w_down,
+):
+    n = lax.axis_size("attn")
+    group = n // EXPERTS
+    rows, width = tokens.shape
+    half = width // 2
+    heads = queries.shape[1] // HEAD_DIM
+    hidden = w_gate.shape[1]
+    blocks = half // TILE
+    slots = n * CAPACITY
+    bf, f32 = jnp.bfloat16, jnp.float32
+    vm, dma = pltpu.VMEM, pltpu.SemaphoreType.DMA
+    anywhere = pl.BlockSpec(memory_space=pl.ANY)
+    return pl.pallas_call(
+        functools.partial(layer_kernel, n),
+        out_shape=(
+            jax.ShapeDtypeStruct(queries.shape, bf),
+            jax.ShapeDtypeStruct(tokens.shape, bf),
+        ),
+        in_specs=[pl.BlockSpec(memory_space=pltpu.SMEM)] + [anywhere] * 11,
+        out_specs=(anywhere, anywhere),
+        scratch_shapes=[
+            vm(queries.shape, bf), vm(new_keys.shape, bf), vm(new_values.shape, bf),
+            vm(key_cache.shape, bf), vm(value_cache.shape, bf), vm(tokens.shape, bf),
+            vm(expert_ids.shape, jnp.int32), vm(gate_weights.shape, f32),
+            vm((rows, heads, HEAD_DIM), f32), vm(new_keys.shape, f32), vm(new_values.shape, f32),
+            vm((rows, heads, HEAD_DIM), f32), vm(queries.shape, bf),
+            vm((EXPERTS, CAPACITY, half), bf), vm((n, CAPACITY, half), bf),
+            vm((n, CAPACITY, half), bf), vm((slots, width), bf), vm((slots, hidden), bf),
+            vm((RING, DEPTH, TILE), bf),
+            vm((blocks, slots, TILE), f32), vm((blocks, slots, TILE), f32),
+            vm((group, EXPERTS * CAPACITY, TILE), f32),
+            vm((blocks, group, EXPERTS, CAPACITY, TILE), bf),
+            vm((blocks, group, EXPERTS, CAPACITY, TILE), bf),
+            vm((blocks, EXPERTS * CAPACITY, TILE), f32),
+            vm((blocks, EXPERTS, CAPACITY, TILE), bf), vm((blocks, EXPERTS, CAPACITY, TILE), bf),
+            vm((rows, EXPERTS * CAPACITY), f32), vm((rows, half), bf),
+            dma((8,)), dma((RING,)), dma((2,)),
+            dma((EXPERTS,)), dma((EXPERTS,)), dma((EXPERTS, group)), dma((n,)), dma((n,)), dma((n,)),
+            dma((blocks,)), dma((blocks,)), dma((blocks, group)), dma((blocks, group)),
+            dma((blocks, EXPERTS)), dma((blocks, EXPERTS)), dma(()), dma(()),
+        ],
+        compiler_params=pltpu.CompilerParams(
+            collective_id=0, has_side_effects=True, vmem_limit_bytes=60 * 1024 * 1024
+        ),
+        name="decode_layer",
+    )(
+        cache_lengths, queries, new_keys, new_values, key_cache, value_cache,
+        tokens, expert_ids, gate_weights, w_gate, w_up, w_down,
+    )
+
+
+def fits(mesh):
+    return mesh.shape["exp"] == 2 and mesh.shape["attn"] == 2 * EXPERTS
+
+
 def solution(mesh):
     placed = (
         P(("groups", "attn"), "exp"),
@@ -122,7 +523,7 @@
         P(("attn", "exp"), None),
     )
     return jax.shard_map(
-        per_device,
+        fused if fits(mesh) else per_device,
         mesh=mesh,
         in_specs=placed,
         out_specs=(P(("groups", "attn"), "exp"), P(("groups", "attn"), None)),

time: 122 us -> 63 us (0.52)
  Pallas kernels: 0 us -> 56.3 us
  matrix products: 35.7 us -> 0 us
  blocking collectives: 29.6 us -> 0 us
  waiting for transfers between devices: 24.7 us -> 0 us
  between operations: 14.2 us -> 0.64 us
  starting transfers between devices: 5.87 us -> 0 us
  other arithmetic: 4.21 us -> 0 us
    pallas_call x0 -> x1, Pallas kernels: none -> 56.3 us  [fused(): pl.pallas_call(functools.partial(layer_kernel, n), out_shape=(jax.ShapeDt...]
    dot_general x7 -> x0, matrix products: 35.7 us -> none  [the longest x1 21 us: per_device(): partial_out = jnp.dot(hidden, w_down, preferred_element_type=jnp.float32)]
    all_to_all x1 -> x0, blocking collectives: 27.2 us -> none  [per_device(): lax.all_to_all(fanned, 'attn', split_axis=0, concat_axis=0, tiled=True)]
    all_to_all x1 -> x0, waiting for transfers between devices: 17.7 us -> none  [per_device(): lax.all_to_all(outbound, 'attn', split_axis=0, concat_axis=0, tiled=True)]
    reduce_scatter x1 -> x0, waiting for transfers between devices: 7 us -> none  [per_device(): lax.psum_scatter(partial_out, 'exp', scatter_dimension=1, tiled=True)]
    all_to_all x1 -> x0, starting transfers between devices: 5.83 us -> none  [per_device(): lax.all_to_all(outbound, 'attn', split_axis=0, concat_axis=0, tiled=True)]
    reshape x5 -> x0, local copies, waits for them, and re-layouts: 5.3 us -> none  [the longest x2 3.86 us: per_device(): partial_out.reshape(attn_devices, core_count, half_slots, model_width)]
    unnamed x14 -> x4, local copies, waits for them, and re-layouts: 0.9 us -> 5.87 us
  transfers between devices with their start and end apart: 2 -> 0, of which waited for: 2 -> 0; matrix products, arithmetic and copies ran while one was open for 3% -> 0% of each run, Pallas kernels for 0% -> 0%
where the time goes in v1:
time: 63 us; the launch traced here: 62.8 us
  Pallas kernels  56.3 us (89%)
  local copies, waits for them, and re-layouts  5.87 us (9%)
  between operations  0.64 us (1%)
    pallas_call x1, Pallas kernels, fused(): pl.pallas_call(functools.partial(layer_kernel, n), out_shape=(jax.ShapeDt...  56.3 us
    unnamed x4, local copies, waits for them, and re-layouts  5.87 us

profile of v1, /device:TPU:0, one launch (start us, length us, event | category | flops | bytes accessed | tf_op | source)
XLA Modules:
  0.0 62.8 jit_solution(1428201898455645940)
XLA Ops:
  0.6 1.4 %copy.14.expert_ids = s32[12,2]{1,0:T(8,128)} copy(s32[12,2]{0,1:T(2,128)} %param.19) | data formatting | bytes 192 | tf_op args[7]
  2.0 1.4 %copy.15.gate_weights = f32[12,2]{1,0:T(8,128)} copy(f32[12,2]{0,1:T(2,128)} %param.20) | data formatting | bytes 192 | tf_op args[8]
  3.3 56.3 %decode_layer.1 = (bf16[12,3072]{1,0:T(8,128)(2,1)}, bf16[12,6144]{1,0:T(8,128)(2,1)}) custom-call(s32[12]{0:T(128)} %lengths.1, bf16[12,3072]{1,0:T(8,128)(2,1)} %queries.1, bf16[12,512]{1,0:T(8,128)(2,1)} %new_keys.1, bf16[12,512]{1,0:T(8,128)(2,1)} %new_values.1, bf16[12,128,512]{2,1,0:T(8,128)(2,1)} %key_cache.1, bf16[12,128,512]{2,1,0:T(8,128)(2,1)} %value_cache.1, ...), custom_call_target="tpu_custom_call" | custom-call | tf_op jit(solution)/shard_map/decode_layer/pallas_call | solution.py:467
  59.7 1.5 %copy.18 = bf16[12,3072]{1,0:T(8,128)(2,1)} copy(bf16[12,3072]{1,0:T(8,128)(2,1)} %get-tuple-element.4) | data formatting | bytes 147456
  61.2 1.6 %copy.19 = bf16[12,6144]{1,0:T(8,128)(2,1)} copy(bf16[12,6144]{1,0:T(8,128)(2,1)} %get-tuple-element.5) | data formatting | bytes 294912

commit v2 on v1

--- a/solution.py
+++ b/solution.py
@@ -14,6 +14,7 @@
 RING = 18
 TILE = 512
 DEPTH = 2048
+LAG = 3
 
 
 def attend(queries, new_keys, new_values, key_cache, value_cache, cache_lengths):
@@ -175,7 +176,7 @@
     q_v, nk_v, nv_v, k_v, v_v, tok_v, ids_v, gw_v,
     qs, nkf, nvf, os, ctx_v,
     outbuf, near, far, x, hid, ring,
-    psend, pgot, tf, tb, yb, zf, zb, home, comb_v, ob,
+    psend, pgot, own_half, tf, tb, yb, zf, zb, home, comb_v, ob,
     in_sem, ring_sem, put_sem,
     d_s, d_r, fy_s, fy_r, fs_s, fs_r,
     p_s, p_r, y_s, y_r, h_s, h_r, o_s, o_r,
@@ -241,22 +242,19 @@
     ids = ids_v[...]
     gates = gw_v[...]
     spots = EXPERTS * CAPACITY
-    lane = lax.broadcasted_iota(jnp.int32, (rows, spots), 1)
-    row_id = lax.broadcasted_iota(jnp.int32, (rows, spots), 0)
-    lane_expert, lane_slot = lane // CAPACITY, lane % CAPACITY
-    first = ids[:, 0:1] == lane_expert
-    second = ids[:, 1:2] == lane_expert
+    spot = lax.broadcasted_iota(jnp.int32, (spots, rows), 0)
+    row_id = lax.broadcasted_iota(jnp.int32, (spots, rows), 1)
+    first = ids[0:1, :] == spot // CAPACITY
+    second = ids[1:2, :] == spot // CAPACITY
     routed = jnp.where(first | second, 1, 0)
-    before = jnp.zeros((rows, spots), jnp.int32)
+    before = jnp.zeros((spots, rows), jnp.int32)
     for r in range(rows - 1):
-        before = before + jnp.where(row_id > r, routed[r : r + 1, :], 0)
-    chosen = (routed > 0) & (before == lane_slot)
-    comb_v[...] = jnp.where(chosen, jnp.where(first, gates[:, 0:1], gates[:, 1:2]), 0.0)
+        before = before + jnp.where(row_id > r, routed[:, r : r + 1], 0)
+    chosen = (routed > 0) & (before == spot % CAPACITY)
+    comb_v[...] = jnp.where(chosen, jnp.where(first, gates[0:1, :], gates[1:2, :]), 0.0)
     selector = jnp.where(chosen, 1.0, 0.0).astype(jnp.bfloat16)
     mine = tok_v[:, pl.ds(pl.multiple_of(c * half, half), half)]
-    outgoing = lax.dot_general(
-        selector, mine, (((0,), (0,)), ((), ())), preferred_element_type=jnp.float32
-    )
+    outgoing = jnp.dot(selector, mine, preferred_element_type=jnp.float32)
     outbuf[...] = outgoing.reshape(EXPERTS, CAPACITY, half).astype(jnp.bfloat16)
     pl.semaphore_wait(barrier, EXPERTS + group - 1)
 
@@ -303,16 +301,14 @@
         sends.append(cp)
 
     pass_on(j * EXPERTS + ex, ex, True)
-    lax.fori_loop(0, rows // at_once, attend_some, 0)
+    third = rows // at_once // 3
+    lax.fori_loop(0, third, attend_some, 0)
     for d in range(1, EXPERTS):
         e2 = (ex + EXPERTS - d) % EXPERTS
         place = j * EXPERTS + e2
         remote(near.at[place], near.at[place], d_s.at[d], d_r.at[e2], {"exp": 1 - c}).wait_recv()
         pass_on(place, e2, True)
-    for h in range(heads):
-        ctx_v[:, h * HEAD_DIM : (h + 1) * HEAD_DIM] = os[:, h, :].astype(jnp.bfloat16)
-    put_context = pltpu.make_async_copy(ctx_v, context, put_sem.at[0])
-    put_context.start()
+    lax.fori_loop(third, 2 * third, attend_some, 0)
     for m in range(1, group):
         j2 = (j + m) % group
         for d in range(EXPERTS):
@@ -322,6 +318,7 @@
                 near.at[place], near.at[place], fy_s.at[e2, m], fy_r.at[place], {"exp": 1 - c}
             ).wait_recv()
             pass_on(place, e2, False)
+    lax.fori_loop(2 * third, rows // at_once, attend_some, 0)
     for place in range(attn_count):
         remote(
             near.at[place], far.at[place], fs_s.at[place], fs_r.at[place], {"exp": 1 - c}
@@ -387,6 +384,15 @@
             to_home(i, d).start()
         home[i, ex] = zb[i, ex]
 
+    def merge(i):
+        sibling(i).wait_recv()
+        mine = own_half[i] + pgot[i]
+        tf[...] = mine.reshape(group, EXPERTS * CAPACITY, TILE)
+        tb[i] = mine.reshape(group, EXPERTS, CAPACITY, TILE).astype(jnp.bfloat16)
+        zf[i] = tf[j]
+        for d in range(1, group):
+            across(i, d).start()
+
     def down_block(i, carry):
         slot, tile = down_tile(i, 0)
         tile.wait()
@@ -394,23 +400,30 @@
         sibling(i).start()
         slot, tile = down_tile(i, 1)
         tile.wait()
-        mine = jnp.dot(hid[...], ring[slot], preferred_element_type=jnp.float32)
-
-        @pl.when(i > 0)
+        own_half[i] = jnp.dot(hid[...], ring[slot], preferred_element_type=jnp.float32)
+
+        @pl.when(i >= 1)
         def _():
-            finish(i - 1)
-
-        sibling(i).wait_recv()
-        mine = mine + pgot[i]
-        tf[...] = mine.reshape(group, EXPERTS * CAPACITY, TILE)
-        tb[i] = mine.reshape(group, EXPERTS, CAPACITY, TILE).astype(jnp.bfloat16)
-        zf[i] = tf[j]
-        for d in range(1, group):
-            across(i, d).start()
+            merge(i - 1)
+
+        @pl.when(i >= LAG)
+        def _():
+            finish(i - LAG)
+
         return carry
 
     lax.fori_loop(0, out_blocks, down_block, 0)
-    finish(out_blocks - 1)
+    merge(out_blocks - 1)
+    for h in range(heads):
+        ctx_v[:, h * HEAD_DIM : (h + 1) * HEAD_DIM] = os[:, h, :].astype(jnp.bfloat16)
+    put_context = pltpu.make_async_copy(ctx_v, context, put_sem.at[0])
+    put_context.start()
+
+    def finish_rest(i, carry):
+        finish(i)
+        return carry
+
+    lax.fori_loop(max(out_blocks - LAG, 0), out_blocks, finish_rest, 0)
 
     def combine(i, carry):
         for d in range(1, EXPERTS):
@@ -418,9 +431,9 @@
             remote(
                 zb.at[i, e2], home.at[i, e2], h_s.at[i, d], h_r.at[i, e2], {"exp": 1 - c}
             ).wait_recv()
-        ob[:, pl.ds(pl.multiple_of(i * TILE, TILE), TILE)] = jnp.dot(
+        ob[:, pl.ds(pl.multiple_of(i * TILE, TILE), TILE)] = lax.dot_general(
             comb_v[...], home[i].astype(jnp.float32).reshape(spots, TILE),
-            precision=lax.Precision.HIGHEST, preferred_element_type=jnp.float32,
+            (((0,), (0,)), ((), ())), precision=lax.Precision.HIGHEST, preferred_element_type=jnp.float32,
         ).astype(jnp.bfloat16)
         return carry
 
@@ -475,19 +488,20 @@
         scratch_shapes=[
             vm(queries.shape, bf), vm(new_keys.shape, bf), vm(new_values.shape, bf),
             vm(key_cache.shape, bf), vm(value_cache.shape, bf), vm(tokens.shape, bf),
-            vm(expert_ids.shape, jnp.int32), vm(gate_weights.shape, f32),
+            vm((2, rows), jnp.int32), vm((2, rows), f32),
             vm((rows, heads, HEAD_DIM), f32), vm(new_keys.shape, f32), vm(new_values.shape, f32),
             vm((rows, heads, HEAD_DIM), f32), vm(queries.shape, bf),
             vm((EXPERTS, CAPACITY, half), bf), vm((n, CAPACITY, half), bf),
             vm((n, CAPACITY, half), bf), vm((slots, width), bf), vm((slots, hidden), bf),
             vm((RING, DEPTH, TILE), bf),
             vm((blocks, slots, TILE), f32), vm((blocks, slots, TILE), f32),
+            vm((blocks, slots, TILE), f32),
             vm((group, EXPERTS * CAPACITY, TILE), f32),
             vm((blocks, group, EXPERTS, CAPACITY, TILE), bf),
             vm((blocks, group, EXPERTS, CAPACITY, TILE), bf),
             vm((blocks, EXPERTS * CAPACITY, TILE), f32),
             vm((blocks, EXPERTS, CAPACITY, TILE), bf), vm((blocks, EXPERTS, CAPACITY, TILE), bf),
-            vm((rows, EXPERTS * CAPACITY), f32), vm((rows, half), bf),
+            vm((EXPERTS * CAPACITY, rows), f32), vm((rows, half), bf),
             dma((8,)), dma((RING,)), dma((2,)),
             dma((EXPERTS,)), dma((EXPERTS,)), dma((EXPERTS, group)), dma((n,)), dma((n,)), dma((n,)),
             dma((blocks,)), dma((blocks,)), dma((blocks, group)), dma((blocks, group)),
@@ -499,7 +513,7 @@
         name="decode_layer",
     )(
         cache_lengths, queries, new_keys, new_values, key_cache, value_cache,
-        tokens, expert_ids, gate_weights, w_gate, w_up, w_down,
+        tokens, expert_ids.T, gate_weights.T, w_gate, w_up, w_down,
     )
 
 

time: 63 us -> 49.3 us (0.78)
  Pallas kernels: 56.3 us -> 45.3 us
  local copies, waits for them, and re-layouts: 5.87 us -> 3.16 us
    pallas_call x1, Pallas kernels: 56.3 us -> 45.3 us  [fused(): pl.pallas_call(functools.partial(layer_kernel, n), out_shape=(jax.ShapeDt...]
    unnamed x4 -> x2, local copies, waits for them, and re-layouts: 5.87 us -> 3.16 us
where the time goes in v2:
time: 49.3 us; the launch traced here: 49.1 us
  Pallas kernels  45.3 us (92%)
  local copies, waits for them, and re-layouts  3.16 us (6%)
  between operations  0.64 us (1%)
    pallas_call x1, Pallas kernels, fused(): pl.pallas_call(functools.partial(layer_kernel, n), out_shape=(jax.ShapeDt...  45.3 us
    unnamed x2, local copies, waits for them, and re-layouts  3.16 us

profile of v2, /device:TPU:0, one launch (start us, length us, event | category | flops | bytes accessed | tf_op | source)
XLA Modules:
  0.0 49.1 jit_solution(14436081707440293985)
XLA Ops:
  0.6 45.3 %decode_layer.1 = (bf16[12,3072]{1,0:T(8,128)(2,1)}, bf16[12,6144]{1,0:T(8,128)(2,1)}) custom-call(s32[12]{0:T(128)} %lengths.1, bf16[12,3072]{1,0:T(8,128)(2,1)} %queries.1, bf16[12,512]{1,0:T(8,128)(2,1)} %new_keys.1, bf16[12,512]{1,0:T(8,128)(2,1)} %new_values.1, bf16[12,128,512]{2,1,0:T(8,128)(2,1)} %key_cache.1, bf16[12,128,512]{2,1,0:T(8,128)(2,1)} %value_cache.1, ...), custom_call_target="tpu_custom_call" | custom-call | tf_op jit(solution)/shard_map/decode_layer/pallas_call | solution.py:480
  45.9 1.5 %copy.16 = bf16[12,3072]{1,0:T(8,128)(2,1)} copy(bf16[12,3072]{1,0:T(8,128)(2,1)} %get-tuple-element.4) | data formatting | bytes 147456
  47.5 1.6 %copy.17 = bf16[12,6144]{1,0:T(8,128)(2,1)} copy(bf16[12,6144]{1,0:T(8,128)(2,1)} %get-tuple-element.5) | data formatting | bytes 294912
